TPU v7x, 32 devices: a whole 2x2x4 slice. The times are simulated.
32 devices in a mesh: dom: 8 (over z, y), feat: 4 (over x, core).
Axes of the slice: x: 2, y: 2, z: 4, core: 2. Of those that a mesh axis runs over, the one named last changes fastest.
Arguments:
- features: bfloat16 [32768, 512], P('dom', 'feat'), may hold values from -6 to 6
- theta: bfloat16 [512, 512], P(None, 'feat'), may hold values from -0.25 to 0.25
- incidence: int32 [3, 4096], P(None, 'dom'), may hold values from 0 to 4095, as said below
- edge_weight: float32 [16384], P('dom'), may hold values from 0.5 to 2
- cotangent: bfloat16 [32768, 512], P('dom', 'feat'), may hold values from -6 to 6
Outputs:
- activation: bfloat16 [32768, 512], P('dom', 'feat')
- grad_features: bfloat16 [32768, 512], P('dom', 'feat')
- grad_theta: float32 [512, 512], P('dom', 'feat')
Inputs may be any that keep to these rules, and one draw needn't show every extreme that they name: `incidence`: in the 64 slots from one vertex owner to one hyperedge owner the live slots (weight over zero) come first, at least one of them; some hyperedge owner receives all 64 slots live from every vertex owner.
All inputs are finite; a program needn't handle non-finite values.
Results may differ from a plain program's by a relative error of at most 0.0073.
Values may be sent and summed in bfloat16 or wider, within the bound.
A program may use at most 64 MiB of HBM per device.

v0:
```python
import jax
import jax.numpy as jnp
from jax import lax
from jax.sharding import PartitionSpec as P


def local(features, theta, incidence, edge_weight, cotangent):
    owners = lax.axis_size("dom")
    nvert = features.shape[0]
    cols = features.shape[1]
    nedge = edge_weight.shape[0]
    vert = incidence[0]
    edge = incidence[1]
    weight = incidence[2]
    weight_f = weight.astype(jnp.float32)
    dvis = lax.rsqrt(1.0 + jax.ops.segment_sum(weight_f, vert, num_segments=nvert))
    slot_scale = weight_f * dvis[vert]
    full_rows = lax.all_gather(features, "feat", axis=1, tiled=True)
    projected = jnp.dot(full_rows, theta, preferred_element_type=jnp.float32).astype(jnp.bfloat16)
    message = (slot_scale[:, None] * projected[vert].astype(jnp.float32)).astype(jnp.bfloat16)
    recv_rows, recv_edge, recv_weight = (
        lax.all_to_all(
            message.reshape(owners, -1, cols), "dom", split_axis=0, concat_axis=0, tiled=True
        ),
        lax.all_to_all(edge.reshape(owners, -1), "dom", split_axis=0, concat_axis=0, tiled=True),
        lax.all_to_all(weight.reshape(owners, -1), "dom", split_axis=0, concat_axis=0, tiled=True),
    )
    recv_edge = recv_edge.reshape(-1)
    degree = 1.0 + jax.ops.segment_sum(
        recv_weight.reshape(-1).astype(jnp.float32), recv_edge, num_segments=nedge
    )
    edge_scale = edge_weight / degree

    def edge_side(rows):
        edge_sum = jax.ops.segment_sum(
            rows.reshape(-1, cols).astype(jnp.float32), recv_edge, num_segments=nedge
        )
        edge_rows = (edge_scale[:, None] * edge_sum).astype(jnp.bfloat16)
        return edge_rows[recv_edge].reshape(owners, -1, cols)

    def vertex_side(back):
        terms = weight_f[:, None] * back.reshape(-1, cols).astype(jnp.float32)
        return dvis[:, None] * jax.ops.segment_sum(terms, vert, num_segments=nvert)

    back = lax.all_to_all(edge_side(recv_rows), "dom", split_axis=0, concat_axis=0, tiled=True)
    summed = vertex_side(back)
    sigma = jax.nn.sigmoid(summed)
    activation = (summed * sigma).astype(jnp.bfloat16)
    slope = sigma * (1.0 + summed * (1.0 - sigma))
    grad_summed = cotangent.astype(jnp.float32) * slope
    grad_message = (slot_scale[:, None] * grad_summed[vert]).astype(jnp.bfloat16)
    grad_recv = lax.all_to_all(
        grad_message.reshape(owners, -1, cols), "dom", split_axis=0, concat_axis=0, tiled=True
    )
    grad_back = lax.all_to_all(edge_side(grad_recv), "dom", split_axis=0, concat_axis=0, tiled=True)
    grad_projected = vertex_side(grad_back).astype(jnp.bfloat16)
    theta_full = lax.all_gather(theta, "feat", axis=1, tiled=True)
    theta_mine = lax.dynamic_slice_in_dim(theta_full, lax.axis_index("feat") * cols, cols, 0)
    grad_total = lax.dot_general(
        lax.all_gather(grad_projected, "feat", axis=1, tiled=True),
        theta_mine,
        (((1,), (1,)), ((), ())),
        preferred_element_type=jnp.float32,
    )
    grad_features = grad_total.astype(jnp.bfloat16)
    share = full_rows.shape[1] // owners
    term = lax.dot_general(
        full_rows, grad_projected, (((0,), (0,)), ((), ())), preferred_element_type=jnp.float32
    )
    total = lax.psum(term, "dom")
    grad_theta = lax.dynamic_slice_in_dim(total, lax.axis_index("dom") * share, share, 0)
    return (activation, grad_features, grad_theta)


def solution(mesh):
    placed = (P("dom", "feat"), P(None, "feat"), P(None, "dom"), P("dom"), P("dom", "feat"))
    return jax.shard_map(
        local,
        mesh=mesh,
        in_specs=placed,
        out_specs=(P("dom", "feat"), P("dom", "feat"), P("dom", "feat")),
        check_vma=False,
    )
```

profile of v0, /device:TPU:0, one launch (start us, length us, event | category | flops | bytes accessed | tf_op | source)
XLA Modules:
  0.0 234.5 jit_solution(12169646869658793668)
XLA Ops:
  7.2 0.7 all-gather.3.cloned.1.call-update
  7.9 0.8 slice_reduce_fusion.1
  8.8 0.7 all_to_all.24
  9.4 7.3 %all-to-all-start = ((s32[8,1,64]{2,1,0:T(1,128)}), s32[8,1,64]{2,1,0:T(1,128)S(1)}, u32[]{:S(2)}, u32[]{:S(2)}) async-start(s32[8,1,64]{2,1,0:T(1,128)} %all_to_all.24), calls=%async_computation | async-start | bytes 8192 | tf_op jit(solution)/shard_map/all_to_all | solution.py:25
  16.7 0.7 compare_select_fusion.1
  17.4 0.7 fusion.19
  18.1 0.7 all_to_all.26
  18.8 4.3 %all-to-all-done = s32[8,1,64]{2,1,0:T(1,128)S(1)} async-done(((s32[8,1,64]{2,1,0:T(1,128)}), s32[8,1,64]{2,1,0:T(1,128)S(1)}, u32[]{:S(2)}, u32[]{:S(2)}) %all-to-all-start) | async-done | bytes 2080 | tf_op jit(solution)/shard_map/all_to_all | solution.py:25
  23.1 3.3 %all-to-all-start.1 = ((s32[8,1,64]{2,1,0:T(1,128)}), s32[8,1,64]{2,1,0:T(1,128)S(1)}, u32[]{:S(2)}, u32[]{:S(2)}) async-start(s32[8,1,64]{2,1,0:T(1,128)} %all_to_all.26), calls=%async_computation.1 | async-start | bytes 8192 | tf_op jit(solution)/shard_map/all_to_all | solution.py:26
  26.4 0.1 convert_element_type.86
  26.5 3.3 %scatter_custom_fusion = f32[4096]{0:T(1024)S(1)} fusion(s32[512]{0:T(512)S(1)} %bitcast.41, f32[512]{0:T(512)S(1)} %bitcast.36, f32[]{:T(128)} %constant.11.clone.1), kind=kCustom, calls=%fused_computation.40 | custom fusion | flops 512 | bytes 16388 | tf_op jit(solution)/shard_map/scatter-add | solution.py:16
  29.8 3.1 %gather_fusion = f32[512]{0:T(512)S(1)} fusion(f32[4096]{0:T(1024)S(1)} %rsqrt.3, s32[1024]{0:T(1024)S(1)} %pad_clamp_fusion.1), kind=kCustom, calls=%fused_computation | custom fusion | bytes 6144 | tf_op jit(solution)/shard_map/gather | solution.py:17
  32.9 0.1 gather.20
  33.0 0.1 broadcast_in_dim_reshape.2
  33.1 0.5 broadcast.109
  33.6 0.7 reduce.21
  34.3 0.1 reshape.181
  34.4 0.1 reshape.183
  34.4 3.3 %scatter_custom_fusion.1 = f32[2048]{0:T(1024)S(1)} fusion(s32[512]{0:T(512)S(1)} %reshape.181, f32[512]{0:T(512)S(1)} %reshape.183, f32[]{:T(128)} %constant.11.clone.1), kind=kCustom, calls=%fused_computation.45 | custom fusion | flops 512 | bytes 8196 | tf_op jit(solution)/shard_map/scatter-add | solution.py:29
  37.7 9.6 %all-gather.3.cloned.1.call-done = bf16[4096,512]{1,0:T(8,128)(2,1)} async-done(((bf16[4096,128]{1,0:T(8,128)(2,1)}), bf16[4096,512]{1,0:T(8,128)(2,1)}) %all-gather.3.cloned.1.call-update) | async-done | bytes 4194320 | tf_op jit(solution)/shard_map/all_gather | solution.py:18
  47.3 3.4 %convolution_convert_fusion.1 = bf16[4096,128]{1,0:T(8,128)(2,1)S(1)} fusion(bf16[4096,512]{1,0:T(8,128)(2,1)} %all-gather.3.cloned.1.call-done, bf16[512,128]{1,0:T(8,128)(2,1)S(1)} %copy-done.2), kind=kOutput, calls=%fused_computation.12 | convolution fusion | flops 537395200 | bytes 5373952 | tf_op jit(solution)/shard_map/dot_general | solution.py:19
  50.8 1.3 gather_fusion.1
  52.1 0.8 fusion.10
  52.9 5.5 %all-to-all-start.2 = ((bf16[8,64,128]{2,1,0:T(8,128)(2,1)}), bf16[8,64,128]{2,1,0:T(8,128)(2,1)S(1)}, u32[]{:S(2)}, u32[]{:S(2)}) async-start(bf16[8,64,128]{2,1,0:T(8,128)(2,1)} %fusion.10), calls=%async_computation.2 | async-start | bytes 262144 | tf_op jit(solution)/shard_map/all_to_all | solution.py:22
  58.5 7.3 %all-to-all-done.2 = bf16[8,64,128]{2,1,0:T(8,128)(2,1)S(1)} async-done(((bf16[8,64,128]{2,1,0:T(8,128)(2,1)}), bf16[8,64,128]{2,1,0:T(8,128)(2,1)S(1)}, u32[]{:S(2)}, u32[]{:S(2)}) %all-to-all-start.2) | async-done | bytes 131104 | tf_op jit(solution)/shard_map/all_to_all | solution.py:22
  65.8 2.5 %scatter_custom_fusion.2 = f32[2048,128]{1,0:T(8,128)S(1)} fusion(s32[512]{0:T(512)S(1)} %reshape.181, f32[]{:T(128)} %constant.12.clone.1, bf16[512,128]{1,0:T(8,128)(2,1)S(1)} %bitcast.28), kind=kCustom, calls=%fused_computation.26 | custom fusion | flops 131072 | bytes 1179652 | tf_op jit(solution)/shard_map/scatter-add | solution.py:35
  68.4 0.3 multiply_convert_fusion.3
  68.7 1.3 gather_fusion.2
  70.1 9.9 %all_to_all.38 = bf16[8,64,128]{2,1,0:T(8,128)(2,1)S(1)} all-to-all(bf16[8,64,128]{2,1,0:T(8,128)(2,1)S(1)} %bitcast.33), channel_id=1, replica_groups=mesh['dom'=8,'feat'=4] {'dom'}, dimensions={0} | all-to-all | bytes 262144 | tf_op jit(solution)/shard_map/all_to_all | solution.py:45
  79.9 3.8 %scatter_custom_fusion.3 = f32[4096,128]{1,0:T(8,128)} fusion(s32[512]{0:T(512)S(1)} %bitcast.42, f32[]{:T(128)} %constant.12.clone.1, bf16[512,128]{1,0:T(8,128)(2,1)S(1)} %bitcast.34, f32[512]{0:T(512)S(1)} %bitcast.37), kind=kCustom, calls=%fused_computation.22 | custom fusion | flops 196608 | bytes 2230276 | tf_op jit(solution)/shard_map/scatter-add | solution.py:43
  83.7 3.2 %multiply_multiply_fusion = (f32[4096,128]{1,0:T(8,128)S(1)}, bf16[4096,128]{1,0:T(8,128)(2,1)}) fusion(bf16[4096,128]{1,0:T(8,128)(2,1)S(1)} %copy-done.1, f32[4096,128]{1,0:T(8,128)} %scatter_custom_fusion.3, f32[4096]{0:T(1024)S(1)} %rsqrt.3), kind=kLoop, calls=%fused_computation.14 | loop fusion | flops 6291456 | bytes 6307840 | tf_op jit(solution)/shard_map/mul | solution.py:50
  86.9 1.0 gather_fusion.3
  87.9 0.1 multiply_convert_fusion.4
  88.1 9.7 %all_to_all.39 = bf16[8,64,128]{2,1,0:T(8,128)(2,1)S(1)} all-to-all(bf16[8,64,128]{2,1,0:T(8,128)(2,1)S(1)} %multiply_convert_fusion.4), channel_id=1, replica_groups=mesh['dom'=8,'feat'=4] {'dom'}, dimensions={0} | all-to-all | bytes 262144 | tf_op jit(solution)/shard_map/all_to_all | solution.py:52
  97.8 2.5 %scatter_custom_fusion.4 = f32[2048,128]{1,0:T(8,128)S(1)} fusion(s32[512]{0:T(512)S(1)} %reshape.181, f32[]{:T(128)} %constant.12.clone.1, bf16[512,128]{1,0:T(8,128)(2,1)S(1)} %bitcast.30), kind=kCustom, calls=%fused_computation.24 | custom fusion | flops 131072 | bytes 1179652 | tf_op jit(solution)/shard_map/scatter-add | solution.py:35
  100.3 0.3 multiply_convert_fusion.2
  100.7 1.3 gather_fusion.4
  102.0 9.7 %all_to_all.40 = bf16[8,64,128]{2,1,0:T(8,128)(2,1)S(1)} all-to-all(bf16[8,64,128]{2,1,0:T(8,128)(2,1)S(1)} %bitcast.31), channel_id=1, replica_groups=mesh['dom'=8,'feat'=4] {'dom'}, dimensions={0} | all-to-all | bytes 262144 | tf_op jit(solution)/shard_map/all_to_all | solution.py:55
  111.7 2.9 %scatter_custom_fusion.5 = f32[4096,128]{1,0:T(8,128)S(1)} fusion(s32[512]{0:T(512)S(1)} %bitcast.43, f32[]{:T(128)} %constant.12.clone.1, bf16[512,128]{1,0:T(8,128)(2,1)S(1)} %bitcast.29, f32[512]{0:T(512)S(1)} %bitcast.38), kind=kCustom, calls=%fused_computation.20 | custom fusion | flops 196608 | bytes 2230276 | tf_op jit(solution)/shard_map/scatter-add | solution.py:43
  114.6 0.7 multiply_convert_fusion
  115.4 4.0 %convolution_bitcast_fusion = f32[512,128]{0,1:T(8,128)} fusion(bf16[4096,128]{1,0:T(8,128)(2,1)S(1)} %multiply_convert_fusion, bf16[4096,512]{1,0:T(8,128)(2,1)} %all-gather.3.cloned.1.call-done), kind=kOutput, calls=%fused_computation.17 | convolution fusion | flops 536870912 | bytes 5505024 | tf_op jit(solution)/shard_map/dot_general | solution.py:67
  119.5 0.7 all-gather.5.cloned.1.call-update
  120.2 6.5 %all_gather.11 = bf16[512,512]{1,0:T(8,128)(2,1)S(1)} all-gather(bf16[512,128]{1,0:T(8,128)(2,1)S(1)} %copy-done.2), channel_id=1, replica_groups=mesh['dom'=8,'feat'=4] {'feat'}, dimensions={1}, use_global_device_ids=true | all-gather | bytes 655360 | tf_op jit(solution)/shard_map/all_gather | solution.py:57
  126.7 60.2 %all-reduce.2.cloned.1.call-done = f32[512,128]{0,1:T(8,128)} async-done(((f32[512,128]{0,1:T(8,128)}), f32[512,128]{0,1:T(8,128)}) %all-reduce.2.cloned.1.call-update) | async-done | bytes 262160 | tf_op jit(solution)/shard_map/psum | solution.py:70
  187.0 0.9 constant_dynamic-slice_fusion
  187.9 0.7 copy.10
  188.6 34.9 %all-gather.5.cloned.1.call-done = bf16[4096,512]{1,0:T(8,128)(2,1)} async-done(((bf16[4096,128]{1,0:T(8,128)(2,1)}), bf16[4096,512]{1,0:T(8,128)(2,1)}) %all-gather.5.cloned.1.call-update) | async-done | bytes 4194320 | tf_op jit(solution)/shard_map/all_gather | solution.py:60
  223.5 4.4 %convolution_convert_fusion = bf16[4096,128]{1,0:T(8,128)(2,1)} fusion(bf16[4096,512]{1,0:T(8,128)(2,1)} %all-gather.5.cloned.1.call-done, bf16[512,512]{1,0:T(8,128)(2,1)S(1)} %all_gather.11, s32[]{:T(128)S(6)} %select_n.31), kind=kOutput, calls=%fused_computation.11 | convolution fusion | flops 537395200 | bytes 5373956 | tf_op jit(solution)/shard_map/dot_general | solution.py:59
  (20 shorter events, 0.2 us)
Async XLA Ops:
  7.2 30.6 %copy-start.3 = (f32[2048]{0:T(1024)S(1)}, f32[2048]{0:T(1024)}, u32[]{:S(2)}) copy-start(f32[2048]{0:T(1024)} %param.8) | copy-start | bytes 24580
  7.2 40.2 %copy-start.2 = (bf16[512,128]{1,0:T(8,128)(2,1)S(1)}, bf16[512,128]{1,0:T(8,128)(2,1)}, u32[]{:S(2)}) copy-start(bf16[512,128]{1,0:T(8,128)(2,1)} %param.6) | copy-start | bytes 393220
  7.2 40.1 %all-gather.3.cloned.1.call-start = ((), (), s32[]{:S(2)}) async-start(), calls=%async_computation.6 | async-start | bytes 5242880 | tf_op jit(solution)/shard_map/all_gather | solution.py:18
  9.4 13.7 %all-to-all-start = ((s32[8,1,64]{2,1,0:T(1,128)}), s32[8,1,64]{2,1,0:T(1,128)S(1)}, u32[]{:S(2)}, u32[]{:S(2)}) async-start(s32[8,1,64]{2,1,0:T(1,128)} %all_to_all.24), calls=%async_computation | async-start | bytes 8192 | tf_op jit(solution)/shard_map/all_to_all | solution.py:25
  23.1 11.3 %all-to-all-start.1 = ((s32[8,1,64]{2,1,0:T(1,128)}), s32[8,1,64]{2,1,0:T(1,128)S(1)}, u32[]{:S(2)}, u32[]{:S(2)}) async-start(s32[8,1,64]{2,1,0:T(1,128)} %all_to_all.26), calls=%async_computation.1 | async-start | bytes 8192 | tf_op jit(solution)/shard_map/all_to_all | solution.py:26
  52.9 12.9 %all-to-all-start.2 = ((bf16[8,64,128]{2,1,0:T(8,128)(2,1)}), bf16[8,64,128]{2,1,0:T(8,128)(2,1)S(1)}, u32[]{:S(2)}, u32[]{:S(2)}) async-start(bf16[8,64,128]{2,1,0:T(8,128)(2,1)} %fusion.10), calls=%async_computation.2 | async-start | bytes 262144 | tf_op jit(solution)/shard_map/all_to_all | solution.py:22
  58.4 128.5 %all-reduce.2.cloned.1.call-start = ((), (), s32[]{:S(2)}) async-start(), calls=%async_computation.8 | async-start | bytes 524288 | tf_op jit(solution)/shard_map/psum | solution.py:70
  68.7 15.0 %copy-start.1 = (bf16[4096,128]{1,0:T(8,128)(2,1)S(1)}, bf16[4096,128]{1,0:T(8,128)(2,1)}, u32[]{:S(2)}) copy-start(bf16[4096,128]{1,0:T(8,128)(2,1)} %param.9) | copy-start | bytes 3145732
  115.4 4.1 %copy-start = (bf16[4096,128]{1,0:T(8,128)(2,1)}, bf16[4096,128]{1,0:T(8,128)(2,1)S(1)}, u32[]{:S(2)}) copy-start(bf16[4096,128]{1,0:T(8,128)(2,1)S(1)} %multiply_convert_fusion) | copy-start | bytes 3145732
  119.4 104.1 %all-gather.5.cloned.1.call-start = ((), (), s32[]{:S(2)}) async-start(), calls=%async_computation.7 | async-start | bytes 5242880 | tf_op jit(solution)/shard_map/all_gather | solution.py:60
Sparse Core Ops, SparseCore 0:
  9.6 37.7 all-gather.2
  119.6 67.3 all-reduce.1
  189.2 34.2 all-gather.4
where the time goes:
time: 235 us; the launch traced here: 234 us
  waiting for transfers between devices  118 us (50%)
  blocking collectives  35.9 us (15%)
  other arithmetic  26.6 us (11%)
  starting transfers between devices  16.2 us (7%)
  between operations  14 us (6%)
  local copies, waits for them, and re-layouts  12.1 us (5%)
  matrix products  11.9 us (5%)
    psum x1, waiting for transfers between devices, local(): total = lax.psum(term, 'dom')  60.2 us
    all_gather x1, waiting for transfers between devices, local(): lax.all_gather(grad_projected, 'feat', axis=1, tiled=True)  34.9 us
    all_to_all x1, blocking collectives, local(): lax.all_to_all(edge_side(recv_rows), 'dom', split_axis=0, concat_axis=0,...  9.85 us
    all_to_all x1, blocking collectives, local(): lax.all_to_all(grad_message.reshape(owners, -1, cols), 'dom', split_axis=...  9.74 us
    all_to_all x1, blocking collectives, local(): lax.all_to_all(edge_side(grad_recv), 'dom', split_axis=0, concat_axis=0,...  9.74 us
    all_gather x1, waiting for transfers between devices, local(): full_rows = lax.all_gather(features, 'feat', axis=1, tiled=True)  9.59 us
    all_to_all x1, waiting for transfers between devices, local(): lax.all_to_all(message.reshape(owners, -1, cols), 'dom', split_axis=0, co...  7.34 us
    all_to_all x1, starting transfers between devices, local(): lax.all_to_all(edge.reshape(owners, -1), 'dom', split_axis=0, concat_axis...  7.28 us
  transfers between devices with their start and end apart: 6, of which 5 were waited for; matrix products, arithmetic and copies ran while one was open for 6% of the time, Pallas kernels for 0%

commit v1 on v0

--- a/solution.py
+++ b/solution.py
@@ -15,7 +15,12 @@
     weight_f = weight.astype(jnp.float32)
     dvis = lax.rsqrt(1.0 + jax.ops.segment_sum(weight_f, vert, num_segments=nvert))
     slot_scale = weight_f * dvis[vert]
-    full_rows = lax.all_gather(features, "feat", axis=1, tiled=True)
+    ring = [features]
+    for hop in range(3):
+        ring.append(lax.ppermute(ring[-1], "feat", [(dev, (dev + 1) % 4) for dev in range(4)]))
+    full_rows = jnp.roll(
+        jnp.concatenate(ring[::-1], axis=1), (lax.axis_index("feat") + 1) * ring[0].shape[1], axis=1
+    )
     projected = jnp.dot(full_rows, theta, preferred_element_type=jnp.float32).astype(jnp.bfloat16)
     message = (slot_scale[:, None] * projected[vert].astype(jnp.float32)).astype(jnp.bfloat16)
     recv_rows, recv_edge, recv_weight = (

time: 235 us -> 223 us (0.949)
  waiting for transfers between devices: 118 us -> 93.9 us
  local copies, waits for them, and re-layouts: 12.1 us -> 20.4 us
    all_gather x1, waiting for transfers between devices: 34.9 us -> 0.01 us  [local(): lax.all_gather(grad_projected, 'feat', axis=1, tiled=True)]
    ppermute x0 -> x3, waiting for transfers between devices: none -> 28.8 us  [local(): lax.ppermute(ring[-1], 'feat', [(dev, (dev + 1) % 4) for dev in range(4)])]
    all_gather x1 -> x0, waiting for transfers between devices: 9.59 us -> none  [local(): full_rows = lax.all_gather(features, 'feat', axis=1, tiled=True)]
    unnamed x9 -> x19, local copies, waits for them, and re-layouts: 0.73 us -> 8.2 us
    all_to_all x1, waiting for transfers between devices: 7.34 us -> 2.94 us  [local(): lax.all_to_all(message.reshape(owners, -1, cols), 'dom', split_axis=0, co...]
    all_to_all x1, waiting for transfers between devices: 4.3 us -> 0.93 us  [local(): lax.all_to_all(edge.reshape(owners, -1), 'dom', split_axis=0, concat_axis...]
  transfers between devices with their start and end apart: 6 -> 8, of which waited for: 5 -> 5; matrix products, arithmetic and copies ran while one was open for 6% -> 11% of each run, Pallas kernels for 0% -> 0%
where the time goes in v1:
time: 223 us; the launch traced here: 222 us
  waiting for transfers between devices  93.9 us (42%)
  blocking collectives  36.9 us (17%)
  other arithmetic  26.7 us (12%)
  local copies, waits for them, and re-layouts  20.4 us (9%)
  starting transfers between devices  18.3 us (8%)
  between operations  15.8 us (7%)
  matrix products  10.2 us (5%)
    psum x1, waiting for transfers between devices, local(): total = lax.psum(term, 'dom')  60.7 us
    ppermute x3, waiting for transfers between devices, local(): lax.ppermute(ring[-1], 'feat', [(dev, (dev + 1) % 4) for dev in range(4)])  28.8 us
    all_to_all x1, blocking collectives, local(): lax.all_to_all(edge_side(recv_rows), 'dom', split_axis=0, concat_axis=0,...  10.2 us
    all_to_all x1, blocking collectives, local(): lax.all_to_all(grad_message.reshape(owners, -1, cols), 'dom', split_axis=...  9.74 us
    all_to_all x1, blocking collectives, local(): lax.all_to_all(edge_side(grad_recv), 'dom', split_axis=0, concat_axis=0,...  9.74 us
    unnamed x19, local copies, waits for them, and re-layouts  8.2 us
    all_gather x1, blocking collectives, local(): theta_full = lax.all_gather(theta, 'feat', axis=1, tiled=True)  7.21 us
    scatter-add x2, other arithmetic, vertex_side(): return dvis[:, None] * jax.ops.segment_sum(terms, vert, num_segments=nvert)  6.73 us
  transfers between devices with their start and end apart: 8, of which 5 were waited for; matrix products, arithmetic and copies ran while one was open for 11% of the time, Pallas kernels for 0%

profile of v1, /device:TPU:0, one launch (start us, length us, event | category | flops | bytes accessed | tf_op | source)
XLA Modules:
  0.0 222.2 jit_solution(14855904490598519930)
XLA Ops:
  8.0 0.5 collective-permute-start
  8.5 14.6 %collective-permute-done = bf16[4096,128]{1,0:T(8,128)(2,1)S(1)} collective-permute-done((bf16[4096,128]{1,0:T(8,128)(2,1)}, bf16[4096,128]{1,0:T(8,128)(2,1)S(1)}, u32[]{:S(2)}, u32[]{:S(2)}) %collective-permute-start) | collective-permute-done | bytes 1048608 | tf_op jit(solution)/shard_map/ppermute | solution.py:20
  23.2 14.2 %collective-permute-done.1 = bf16[4096,128]{1,0:T(8,128)(2,1)S(1)} collective-permute-done((bf16[4096,128]{1,0:T(8,128)(2,1)S(1)}, bf16[4096,128]{1,0:T(8,128)(2,1)S(1)}, u32[]{:S(2)}, u32[]{:S(2)}) %collective-permute-start.1) | collective-permute-done | bytes 1048608 | tf_op jit(solution)/shard_map/ppermute | solution.py:20
  37.4 0.8 slice_reduce_fusion.1
  38.2 0.7 all_to_all.24
  38.9 6.6 %all-to-all-start = ((s32[8,1,64]{2,1,0:T(1,128)}), s32[8,1,64]{2,1,0:T(1,128)S(1)}, u32[]{:S(2)}, u32[]{:S(2)}) async-start(s32[8,1,64]{2,1,0:T(1,128)} %all_to_all.24), calls=%async_computation | async-start | bytes 8192 | tf_op jit(solution)/shard_map/all_to_all | solution.py:30
  45.5 0.7 compare_select_fusion.1
  46.2 0.7 fusion.24
  46.9 3.3 %scatter_custom_fusion = f32[4096]{0:T(1024)S(1)} fusion(s32[512]{0:T(512)S(1)} %bitcast.37, f32[512]{0:T(512)S(1)} %bitcast.32, f32[]{:T(128)} %constant.16.clone.1), kind=kCustom, calls=%fused_computation.50 | custom fusion | flops 512 | bytes 16388 | tf_op jit(solution)/shard_map/scatter-add | solution.py:16
  50.3 0.7 all_to_all.26
  51.0 0.9 all-to-all-done
  51.9 5.1 %all-to-all-start.1 = ((s32[8,1,64]{2,1,0:T(1,128)}), s32[8,1,64]{2,1,0:T(1,128)S(1)}, u32[]{:S(2)}, u32[]{:S(2)}) async-start(s32[8,1,64]{2,1,0:T(1,128)} %all_to_all.26), calls=%async_computation.1 | async-start | bytes 8192 | tf_op jit(solution)/shard_map/all_to_all | solution.py:31
  57.1 3.1 %gather_fusion = f32[512]{0:T(512)S(1)} fusion(f32[4096]{0:T(1024)S(1)} %rsqrt.3, s32[1024]{0:T(1024)S(1)} %get-tuple-element.10), kind=kCustom, calls=%fused_computation | custom fusion | bytes 6144 | tf_op jit(solution)/shard_map/gather | solution.py:17
  60.3 1.5 constant_dynamic-update-slice_fusion.7
  61.8 0.4 constant_dynamic-update-slice_fusion.6
  62.2 0.4 constant_dynamic-update-slice_fusion.5
  62.6 0.4 constant_dynamic-update-slice_fusion.4
  63.0 1.6 constant_dynamic-update-slice_fusion.3
  64.6 0.4 constant_dynamic-update-slice_fusion.2
  65.0 0.4 constant_dynamic-update-slice_fusion.1
  65.3 0.4 constant_dynamic-update-slice_fusion
  65.7 3.2 %copy-done.2 = bf16[4096,1024]{1,0:T(8,128)(2,1)} copy-done((bf16[4096,1024]{1,0:T(8,128)(2,1)}, bf16[4096,1024]{1,0:T(8,128)(2,1)S(1)}, u32[]{:S(2)}) %copy-start.2) | copy-done | bytes 8388632
  68.9 1.3 convolution_convert_fusion.1
  70.2 1.3 gather_fusion.1
  71.6 0.8 fusion.13
  72.4 6.0 %all-to-all-start.2 = ((bf16[8,64,128]{2,1,0:T(8,128)(2,1)}), bf16[8,64,128]{2,1,0:T(8,128)(2,1)S(1)}, u32[]{:S(2)}, u32[]{:S(2)}) async-start(bf16[8,64,128]{2,1,0:T(8,128)(2,1)} %fusion.13), calls=%async_computation.2 | async-start | bytes 262144 | tf_op jit(solution)/shard_map/all_to_all | solution.py:27
  78.4 0.5 broadcast.110
  78.9 0.7 reduce.21
  79.7 3.3 %scatter_custom_fusion.1 = f32[2048]{0:T(1024)S(1)} fusion(s32[512]{0:T(512)S(1)} %reshape.181, f32[512]{0:T(512)S(1)} %reshape.183, f32[]{:T(128)} %constant.16.clone.1), kind=kCustom, calls=%fused_computation.55 | custom fusion | flops 512 | bytes 8196 | tf_op jit(solution)/shard_map/scatter-add | solution.py:34
  83.0 2.9 %all-to-all-done.2 = bf16[8,64,128]{2,1,0:T(8,128)(2,1)S(1)} async-done(((bf16[8,64,128]{2,1,0:T(8,128)(2,1)}), bf16[8,64,128]{2,1,0:T(8,128)(2,1)S(1)}, u32[]{:S(2)}, u32[]{:S(2)}) %all-to-all-start.2) | async-done | bytes 131104 | tf_op jit(solution)/shard_map/all_to_all | solution.py:27
  86.0 2.5 %scatter_custom_fusion.2 = f32[2048,128]{1,0:T(8,128)S(1)} fusion(s32[512]{0:T(512)S(1)} %reshape.181, f32[]{:T(128)} %constant.17.clone.1, bf16[512,128]{1,0:T(8,128)(2,1)S(1)} %bitcast.24), kind=kCustom, calls=%fused_computation.28 | custom fusion | flops 131072 | bytes 1179652 | tf_op jit(solution)/shard_map/scatter-add | solution.py:40
  88.8 1.3 gather_fusion.2
  90.2 10.2 %all_to_all.38 = bf16[8,64,128]{2,1,0:T(8,128)(2,1)S(1)} all-to-all(bf16[8,64,128]{2,1,0:T(8,128)(2,1)S(1)} %bitcast.29), channel_id=1, replica_groups=mesh['dom'=8,'feat'=4] {'dom'}, dimensions={0} | all-to-all | bytes 262144 | tf_op jit(solution)/shard_map/all_to_all | solution.py:50
  100.4 3.9 %scatter_custom_fusion.3 = f32[4096,128]{1,0:T(8,128)} fusion(s32[512]{0:T(512)S(1)} %bitcast.38, f32[]{:T(128)} %constant.17.clone.1, bf16[512,128]{1,0:T(8,128)(2,1)S(1)} %bitcast.30, f32[512]{0:T(512)S(1)} %bitcast.33), kind=kCustom, calls=%fused_computation.24 | custom fusion | flops 196608 | bytes 2230276 | tf_op jit(solution)/shard_map/scatter-add | solution.py:48
  104.2 3.1 %multiply_multiply_fusion = (f32[4096,128]{1,0:T(8,128)S(1)}, bf16[4096,128]{1,0:T(8,128)(2,1)}) fusion(bf16[4096,128]{1,0:T(8,128)(2,1)S(1)} %copy-done.3, f32[4096,128]{1,0:T(8,128)} %scatter_custom_fusion.3, f32[4096]{0:T(1024)S(1)} %rsqrt.3), kind=kLoop, calls=%fused_computation.17 | loop fusion | flops 6291456 | bytes 6307840 | tf_op jit(solution)/shard_map/mul | solution.py:55
  107.4 1.0 gather_fusion.3
  108.5 9.7 %all_to_all.39 = bf16[8,64,128]{2,1,0:T(8,128)(2,1)S(1)} all-to-all(bf16[8,64,128]{2,1,0:T(8,128)(2,1)S(1)} %multiply_convert_fusion.4), channel_id=1, replica_groups=mesh['dom'=8,'feat'=4] {'dom'}, dimensions={0} | all-to-all | bytes 262144 | tf_op jit(solution)/shard_map/all_to_all | solution.py:57
  118.3 2.5 %scatter_custom_fusion.4 = f32[2048,128]{1,0:T(8,128)S(1)} fusion(s32[512]{0:T(512)S(1)} %reshape.181, f32[]{:T(128)} %constant.17.clone.1, bf16[512,128]{1,0:T(8,128)(2,1)S(1)} %bitcast.26), kind=kCustom, calls=%fused_computation.26 | custom fusion | flops 131072 | bytes 1179652 | tf_op jit(solution)/shard_map/scatter-add | solution.py:40
  121.2 1.3 gather_fusion.4
  122.5 9.7 %all_to_all.40 = bf16[8,64,128]{2,1,0:T(8,128)(2,1)S(1)} all-to-all(bf16[8,64,128]{2,1,0:T(8,128)(2,1)S(1)} %bitcast.27), channel_id=1, replica_groups=mesh['dom'=8,'feat'=4] {'dom'}, dimensions={0} | all-to-all | bytes 262144 | tf_op jit(solution)/shard_map/all_to_all | solution.py:60
  132.2 2.9 %scatter_custom_fusion.5 = f32[4096,128]{1,0:T(8,128)S(1)} fusion(s32[512]{0:T(512)S(1)} %bitcast.39, f32[]{:T(128)} %constant.17.clone.1, bf16[512,128]{1,0:T(8,128)(2,1)S(1)} %bitcast.25, f32[512]{0:T(512)S(1)} %bitcast.34), kind=kCustom, calls=%fused_computation.22 | custom fusion | flops 196608 | bytes 2230276 | tf_op jit(solution)/shard_map/scatter-add | solution.py:48
  135.1 0.7 multiply_convert_fusion
  135.9 4.6 %fusion = f32[512,128]{1,0:T(8,128)} fusion(bf16[4096,128]{1,0:T(8,128)(2,1)S(1)} %multiply_convert_fusion, bf16[4096,1024]{1,0:T(8,128)(2,1)} %copy-done.2, s32[]{:T(128)S(6)} %select_n.44), kind=kOutput, calls=%fused_computation.13 | convolution fusion | flops 536870912 | bytes 5505028 | tf_op jit(solution)/shard_map/dot_general | solution.py:72
  140.5 0.5 all-gather.2.cloned.1.call-update
  141.0 7.2 %all_gather.7 = bf16[512,512]{1,0:T(8,128)(2,1)S(1)} all-gather(bf16[512,128]{1,0:T(8,128)(2,1)S(1)} %copy-done.4), channel_id=1, replica_groups=mesh['dom'=8,'feat'=4] {'feat'}, dimensions={1}, use_global_device_ids=true | all-gather | bytes 655360 | tf_op jit(solution)/shard_map/all_gather | solution.py:62
  148.2 60.7 %all-reduce.2.cloned.1.call-done = f32[512,128]{1,0:T(8,128)} async-done(((f32[512,128]{1,0:T(8,128)}), f32[512,128]{1,0:T(8,128)}) %all-reduce.2.cloned.1.call-update) | async-done | bytes 262160 | tf_op jit(solution)/shard_map/psum | solution.py:75
  209.0 1.4 constant_dynamic-slice_fusion
  210.3 4.4 %convolution_convert_fusion = bf16[4096,128]{1,0:T(8,128)(2,1)} fusion(bf16[4096,512]{1,0:T(8,128)(2,1)} %all-gather.2.cloned.1.call-done, bf16[512,512]{1,0:T(8,128)(2,1)S(1)} %all_gather.7, s32[]{:T(128)S(6)} %select_n.46), kind=kOutput, calls=%fused_computation.11 | convolution fusion | flops 537395200 | bytes 5373956 | tf_op jit(solution)/shard_map/dot_general | solution.py:64
  (33 shorter events, 1.4 us)
Async XLA Ops:
  8.0 15.1 %collective-permute-start = (bf16[4096,128]{1,0:T(8,128)(2,1)}, bf16[4096,128]{1,0:T(8,128)(2,1)S(1)}, u32[]{:S(2)}, u32[]{:S(2)}) collective-permute-start(bf16[4096,128]{1,0:T(8,128)(2,1)} %param.5), channel_id=1, source_target_pairs={{0,1},{1,2},{2,3},{3,0},{4,5},{5,6},{6,7},{7,4},{8,9},{9,10},{10,1... | collective-permute-start | bytes 3145736 | tf_op jit(solution)/shard_map/ppermute | solution.py:20
  23.1 14.2 %collective-permute-start.1 = (bf16[4096,128]{1,0:T(8,128)(2,1)S(1)}, bf16[4096,128]{1,0:T(8,128)(2,1)S(1)}, u32[]{:S(2)}, u32[]{:S(2)}) collective-permute-start(bf16[4096,128]{1,0:T(8,128)(2,1)S(1)} %collective-permute-done), channel_id=1, source_target_pairs={{0,1},{1,2},{2,3},{3,0},{4,5},{5,6},{6,7},{7,4},{8,9},{9,10},{10,1... | collective-permute-start | bytes 3145736 | tf_op jit(solution)/shard_map/ppermute | solution.py:20
  37.3 23.0 %collective-permute-start.2 = (bf16[4096,128]{1,0:T(8,128)(2,1)S(1)}, bf16[4096,128]{1,0:T(8,128)(2,1)}, u32[]{:S(2)}, u32[]{:S(2)}) collective-permute-start(bf16[4096,128]{1,0:T(8,128)(2,1)S(1)} %collective-permute-done.1), channel_id=1, source_target_pairs={{0,1},{1,2},{2,3},{3,0},{4,5},{5,6},{6,7},{7,4},{8,9},{9,10},{10,1... | collective-permute-start | bytes 3145736 | tf_op jit(solution)/shard_map/ppermute | solution.py:20
  38.9 13.0 %all-to-all-start = ((s32[8,1,64]{2,1,0:T(1,128)}), s32[8,1,64]{2,1,0:T(1,128)S(1)}, u32[]{:S(2)}, u32[]{:S(2)}) async-start(s32[8,1,64]{2,1,0:T(1,128)} %all_to_all.24), calls=%async_computation | async-start | bytes 8192 | tf_op jit(solution)/shard_map/all_to_all | solution.py:30
  51.9 20.5 %all-to-all-start.1 = ((s32[8,1,64]{2,1,0:T(1,128)}), s32[8,1,64]{2,1,0:T(1,128)S(1)}, u32[]{:S(2)}, u32[]{:S(2)}) async-start(s32[8,1,64]{2,1,0:T(1,128)} %all_to_all.26), calls=%async_computation.1 | async-start | bytes 8192 | tf_op jit(solution)/shard_map/all_to_all | solution.py:31
  57.1 5.5 %copy-start.1 = (bf16[4096,128]{1,0:T(8,128)(2,1)S(1)}, bf16[4096,128]{1,0:T(8,128)(2,1)}, u32[]{:S(2)}) copy-start(bf16[4096,128]{1,0:T(8,128)(2,1)} %param.5) | copy-start | bytes 3145732
  63.0 6.0 %copy-start.4 = (bf16[512,128]{1,0:T(8,128)(2,1)S(1)}, bf16[512,128]{1,0:T(8,128)(2,1)}, u32[]{:S(2)}) copy-start(bf16[512,128]{1,0:T(8,128)(2,1)} %param.6) | copy-start | bytes 393220
  65.7 3.2 %copy-start.2 = (bf16[4096,1024]{1,0:T(8,128)(2,1)}, bf16[4096,1024]{1,0:T(8,128)(2,1)S(1)}, u32[]{:S(2)}) copy-start(bf16[4096,1024]{1,0:T(8,128)(2,1)S(1)} %constant_dynamic-update-slice_fusion) | copy-start | bytes 25165828
  68.9 14.1 %copy-start.5 = (f32[2048]{0:T(1024)S(1)}, f32[2048]{0:T(1024)}, u32[]{:S(2)}) copy-start(f32[2048]{0:T(1024)} %param.8) | copy-start | bytes 24580
  70.2 34.0 %copy-start.3 = (bf16[4096,128]{1,0:T(8,128)(2,1)S(1)}, bf16[4096,128]{1,0:T(8,128)(2,1)}, u32[]{:S(2)}) copy-start(bf16[4096,128]{1,0:T(8,128)(2,1)} %param.9) | copy-start | bytes 3145732
  72.4 13.6 %all-to-all-start.2 = ((bf16[8,64,128]{2,1,0:T(8,128)(2,1)}), bf16[8,64,128]{2,1,0:T(8,128)(2,1)S(1)}, u32[]{:S(2)}, u32[]{:S(2)}) async-start(bf16[8,64,128]{2,1,0:T(8,128)(2,1)} %fusion.13), calls=%async_computation.2 | async-start | bytes 262144 | tf_op jit(solution)/shard_map/all_to_all | solution.py:27
  78.4 130.6 %all-reduce.2.cloned.1.call-start = ((), (), s32[]{:S(2)}) async-start(), calls=%async_computation.7 | async-start | bytes 524288 | tf_op jit(solution)/shard_map/psum | solution.py:75
  135.8 4.7 %copy-start = (bf16[4096,128]{1,0:T(8,128)(2,1)}, bf16[4096,128]{1,0:T(8,128)(2,1)S(1)}, u32[]{:S(2)}) copy-start(bf16[4096,128]{1,0:T(8,128)(2,1)S(1)} %multiply_convert_fusion) | copy-start | bytes 3145732
  140.4 69.9 %all-gather.2.cloned.1.call-start = ((), (), s32[]{:S(2)}) async-start(), calls=%async_computation.6 | async-start | bytes 5242880 | tf_op jit(solution)/shard_map/all_gather | solution.py:65
Sparse Core Ops, SparseCore 0:
  140.6 68.3 all-reduce.1
Sparse Core Ops, SparseCore 1:
  143.0 32.7 all-gather.1
